TPU v7x, 32 devices: a whole 2x2x4 slice. The times are simulated.
32 devices in a mesh: row: 4 (over y, x), rhs: 8 (over z, core).
Axes of the slice: x: 2, y: 2, z: 4, core: 2. Of those that a mesh axis runs over, the one named last changes fastest.
Arguments:
- factor: bfloat16 [2, 2048, 512], P(None, 'row', 'rhs'), may hold values from -0.25 to 0.25
- pivots: float32 [2, 512], replicated, may hold values from 2 to 3
- right_sides: float32 [2048, 1024], P('row', 'rhs'), may hold values from -6 to 6
Outputs:
- solved: float32 [2048, 1024], P('row', 'rhs')
All inputs are finite; a program needn't handle non-finite values.
Results may differ from a plain program's by a relative error of at most 0.0003.
Values may be sent and summed in bfloat16 or wider, within the bound.
A program may use at most 64 MiB of HBM per device.

v0:
```python
import jax
import jax.numpy as jnp
from jax import lax
from jax.sharding import PartitionSpec as P


def broadcast(value, axis, source):
    kept = jnp.where(lax.axis_index(axis) == source, value, 0).astype(value.dtype)
    return lax.psum(kept, axis)


def solve_block(panel_rows, pivot_row, resid_rows):
    block = panel_rows.astype(jnp.float32)
    diag_k = jnp.tril(block, -1) + jnp.diag(pivot_row)
    return lax.linalg.triangular_solve(diag_k, resid_rows, left_side=True, lower=True)


def spread(candidate, owner):
    return broadcast(candidate, "row", owner)


def advance(resid, panel, solved_rows, global_row, index, offset):
    width = solved_rows.shape[0]
    update = jnp.dot(
        panel.astype(jnp.float32),
        solved_rows,
        precision=lax.Precision.HIGHEST,
        preferred_element_type=jnp.float32,
    )
    placed = resid.at[offset : offset + width].set(solved_rows)
    inside = (global_row >= index * width) & (global_row < (index + 1) * width)
    lower = global_row >= (index + 1) * width
    return jnp.where(lower, resid - update, jnp.where(inside, placed, resid))


def body(factor, pivots, right_sides):
    rows = right_sides.shape[0]
    width = pivots.shape[1]
    count = pivots.shape[0]
    global_row = lax.axis_index("row") * rows + lax.broadcasted_iota(jnp.int32, (rows, 1), 0)
    every_panel = lax.all_gather(factor, "rhs", axis=2, tiled=True)
    resid = right_sides
    for index in range(count):
        panel = every_panel[index]
        owner = index * width // rows
        offset = index * width % rows
        candidate = solve_block(panel, pivots[index], resid)
        solved_rows = spread(candidate, owner)
        resid = advance(resid, panel, solved_rows, global_row, index, offset)
    return resid


def solution(mesh):
    in_specs = (P(None, "row", "rhs"), P(), P("row", "rhs"))
    out_specs = P("row", "rhs")
    return jax.shard_map(body, mesh=mesh, in_specs=in_specs, out_specs=out_specs, check_vma=False)
```

profile of v0, /device:TPU:4, one launch (start us, length us, event | category | flops | bytes accessed | tf_op | source)
XLA Modules:
  0.0 197.8 jit_solution(2651999364103907706)
XLA Ops:
  6.5 1.7 copy.13
  8.4 0.6 copy-done.2
  9.0 23.3 %all-gather.2.cloned.1.call-done = bf16[2,512,512]{1,0,2:T(2,128)(2,1)} async-done(((bf16[2,512,64]{1,0,2:T(2,128)(2,1)}), bf16[2,512,512]{1,0,2:T(2,128)(2,1)}) %all-gather.2.cloned.1.call-update) | async-done | bytes 1048592 | tf_op jit(solution)/shard_map/all_gather | solution.py:41
  32.3 3.3 %fusion.53 = (bf16[1,512,512]{1,0,2:T(2,128)(2,1)S(1)}, bf16[1,512,512]{1,0,2:T(2,128)(2,1)S(1)}) fusion(bf16[2,512,512]{1,0,2:T(2,128)(2,1)} %all-gather.2.cloned.1.call-done), kind=kLoop, calls=%fused_computation.81 | loop fusion | bytes 2097152 | tf_op jit(solution)/shard_map/slice | solution.py:44
  35.6 1.3 copy.20
  36.9 1.3 copy.21
  38.2 0.4 fusion.4
  38.7 0.7 broadcast.124.clone
  39.4 10.5 %while.8 = (s32[]{:T(128)}, f32[512,512]{1,0:T(8,128)S(1)}, s32[4,2]{0,1:T(2,128)S(1)}, f32[4,128,128]{2,1,0:T(8,128)}, s32[]{:T(128)}) while((s32[]{:T(128)}, f32[512,512]{1,0:T(8,128)S(1)}, s32[4,2]{0,1:T(2,128)S(1)}, f32[4,128,128]{2,1,0:T(8,128)}, s32[]{:T(128)}) %tuple.56), condition=%wide.while_cond.2, body=%wide.while_body.2.sunk | while | flops 2 | bytes 132705 | solution.py:15
  39.5 0.6 fusion.67
  40.0 2.0 %bitcast_dynamic-update-slice_fusion.4 = f32[4,128,128]{2,1,0:T(8,128)} fusion(f32[4,128,128]{2,1,0:T(8,128)} %get-tuple-element.166, s32[]{:T(128)} %get-tuple-element.163, f32[512,512]{1,0:T(8,128)S(1)} %get-tuple-element.169, s32[]{:T(128)} %bitcast.71, s32[]{:T(128)} %bitcast.72), kind=kLoop, calls=%fused_computation.clone.1 | loop fusion | bytes 132608 | tf_op jit(solution)/shard_map/triangular_solve | solution.py:15
  42.1 0.6 fusion.67
  42.7 2.0 %bitcast_dynamic-update-slice_fusion.4 = f32[4,128,128]{2,1,0:T(8,128)} fusion(f32[4,128,128]{2,1,0:T(8,128)} %get-tuple-element.166, s32[]{:T(128)} %get-tuple-element.163, f32[512,512]{1,0:T(8,128)S(1)} %get-tuple-element.169, s32[]{:T(128)} %bitcast.71, s32[]{:T(128)} %bitcast.72), kind=kLoop, calls=%fused_computation.clone.1 | loop fusion | bytes 132608 | tf_op jit(solution)/shard_map/triangular_solve | solution.py:15
  44.7 0.6 fusion.67
  45.3 2.0 %bitcast_dynamic-update-slice_fusion.4 = f32[4,128,128]{2,1,0:T(8,128)} fusion(f32[4,128,128]{2,1,0:T(8,128)} %get-tuple-element.166, s32[]{:T(128)} %get-tuple-element.163, f32[512,512]{1,0:T(8,128)S(1)} %get-tuple-element.169, s32[]{:T(128)} %bitcast.71, s32[]{:T(128)} %bitcast.72), kind=kLoop, calls=%fused_computation.clone.1 | loop fusion | bytes 132608 | tf_op jit(solution)/shard_map/triangular_solve | solution.py:15
  47.4 0.6 fusion.67
  47.9 2.0 %bitcast_dynamic-update-slice_fusion.4 = f32[4,128,128]{2,1,0:T(8,128)} fusion(f32[4,128,128]{2,1,0:T(8,128)} %get-tuple-element.166, s32[]{:T(128)} %get-tuple-element.163, f32[512,512]{1,0:T(8,128)S(1)} %get-tuple-element.169, s32[]{:T(128)} %bitcast.71, s32[]{:T(128)} %bitcast.72), kind=kLoop, calls=%fused_computation.clone.1 | loop fusion | bytes 132608 | tf_op jit(solution)/shard_map/triangular_solve | solution.py:15
  49.9 40.7 %custom-call.4 = f32[4,128,128]{1,2,0:T(8,128)} custom-call(f32[4,128,128]{2,1,0:T(8,128)} %get-tuple-element.60), custom_call_target="InvertDiagBlocksLowerTriangular" | custom-call | tf_op jit(solution)/shard_map/triangular_solve/custom-call.1 | solution.py:15
  90.7 1.2 fusion.38
  91.9 0.2 convolution_subtract_fusion.3
  92.1 0.3 fusion.37
  92.4 0.3 convolution_subtract_fusion.2
  92.6 0.3 fusion.35
  92.9 0.3 convolution_subtract_fusion.5
  93.3 0.3 fusion.34
  93.6 0.7 maximum_select_fusion
  94.4 8.2 %while.9 = (s32[]{:T(128)}, f32[512,512]{1,0:T(8,128)S(1)}, s32[4,2]{0,1:T(2,128)S(1)}, f32[4,128,128]{2,1,0:T(8,128)S(1)}, s32[]{:T(128)}) while((s32[]{:T(128)}, f32[512,512]{1,0:T(8,128)S(1)}, s32[4,2]{0,1:T(2,128)S(1)}, f32[4,128,128]{2,1,0:T(8,128)S(1)}, s32[]{:T(128)}) %tuple.68), condition=%wide.while_cond.2.clone, body=%wide.while_body.2.clone.sunk | while | flops 2 | bytes 131181 | solution.py:15
  94.4 0.1 constant_dynamic-slice_fusion.5
  94.5 0.6 fusion.68
  95.1 1.3 bitcast_dynamic-update-slice_fusion.5
  96.5 0.6 fusion.68
  97.1 1.3 bitcast_dynamic-update-slice_fusion.5
  98.6 0.6 fusion.68
  99.2 1.3 bitcast_dynamic-update-slice_fusion.5
  100.6 0.6 fusion.68
  101.2 1.3 bitcast_dynamic-update-slice_fusion.5
  102.6 39.3 %custom-call.5 = f32[4,128,128]{1,2,0:T(8,128)S(1)} custom-call(f32[4,128,128]{2,1,0:T(8,128)S(1)} %get-tuple-element.61), custom_call_target="InvertDiagBlocksLowerTriangular" | custom-call | tf_op jit(solution)/shard_map/triangular_solve/custom-call.1 | solution.py:15
  141.9 1.6 fusion.2
  143.6 0.3 fusion.32
  143.9 0.2 convolution_subtract_fusion.1
  144.1 0.3 fusion.31
  144.4 0.3 convolution_subtract_fusion
  144.6 0.3 fusion.29
  144.9 0.3 convolution_subtract_fusion.4
  145.2 0.3 fusion.28
  145.5 0.7 maximum_select_fusion.1
  146.3 42.6 %all-reduce.5.cloned.1.call-done = f32[512,128]{1,0:T(8,128)} async-done(((f32[512,128]{1,0:T(8,128)}), f32[512,128]{1,0:T(8,128)}) %all-reduce.5.cloned.1.call-update) | async-done | bytes 262160 | tf_op jit(solution)/shard_map/psum | solution.py:9
  188.9 2.3 %fusion.3 = f32[512,128]{1,0:T(8,128)} fusion(f32[512,128]{1,0:T(8,128)S(1)} %fusion.2, f32[512,128]{1,0:T(8,128)} %all-reduce.5.cloned.1.call-done, bf16[1,512,512]{2,1,0:T(8,128)(2,1)S(1)} %copy.21, pred[512]{0:T(512)(128)(4,1)S(1)} %get-tuple-element.99, pred[512]{0:T(512)(128)(4,1)S(1)} %get-tuple-element.98), kind=kOutput, calls=%fused_computation.9 | convolution fusion | flops 402849792 | bytes 1311744 | tf_op jit(solution)/shard_map/dot_general | solution.py:24
  (26 shorter events, 0.7 us)
Async XLA Ops:
  6.5 25.7 %all-gather.2.cloned.1.call-start = ((), (), s32[]{:S(2)}) async-start(), calls=%async_computation | async-start | bytes 1179648 | tf_op jit(solution)/shard_map/all_gather | solution.py:41
  8.3 133.7 %all-reduce.3.cloned.1.call-start = ((), (), s32[]{:S(2)}) async-start(), calls=%async_computation.1 | async-start | bytes 524288 | tf_op jit(solution)/shard_map/psum | solution.py:9
  8.3 0.7 copy-start.2
  38.6 52.0 %copy-start = (f32[512,128]{1,0:T(8,128)S(1)}, f32[512,128]{1,0:T(8,128)}, u32[]{:S(2)}) copy-start(f32[512,128]{1,0:T(8,128)} %param.15) | copy-start | bytes 786436
  90.7 1.4 copy-start.1
  94.3 94.6 %all-reduce.5.cloned.1.call-start = ((), (), s32[]{:S(2)}) async-start(), calls=%async_computation.2 | async-start | bytes 524288 | tf_op jit(solution)/shard_map/psum | solution.py:9
Sparse Core Ops, SparseCore 0:
  9.0 23.2 all-gather.1
  94.4 43.1 all-reduce.2
  146.4 42.4 all-reduce.4
where the time goes:
time: 200 us; the launch traced here: 198 us
  other arithmetic  81.9 us (41%)
  waiting for transfers between devices  65.9 us (33%)
  local copies, waits for them, and re-layouts  27.6 us (14%)
  between operations  13.4 us (7%)
  matrix products  8.71 us (4%)
    another operation x4, other arithmetic, solve_block(): lax.linalg.triangular_solve(diag_k, resid_rows, left_side=True, lower=True)  80.5 us
    psum x2, waiting for transfers between devices, broadcast(): return lax.psum(kept, axis)  42.6 us
    all_gather x1, waiting for transfers between devices, body(): every_panel = lax.all_gather(factor, 'rhs', axis=2, tiled=True)  23.3 us
    another operation x27, local copies, waits for them, and re-layouts, solve_block(): lax.linalg.triangular_solve(diag_k, resid_rows, left_side=True, lower=True)  19.4 us
    unnamed x9, local copies, waits for them, and re-layouts  4.98 us
    another operation x14, matrix products, solve_block(): lax.linalg.triangular_solve(diag_k, resid_rows, left_side=True, lower=True)  4.75 us
  transfers between devices with their start and end apart: 3, of which 2 were waited for; matrix products, arithmetic and copies ran while one was open for 24% of the time, Pallas kernels for 0%

commit v1 on v0

v1 whole, which is shorter than its diff:
```python
import functools

import jax
import jax.numpy as jnp
from jax import lax
from jax.experimental import pallas as pl
from jax.experimental.pallas import tpu as pltpu
from jax.sharding import PartitionSpec as P

F32 = jnp.float32
BF16 = jnp.bfloat16
CORES = 2
LANES = 128
BASE = 16


def dot(a, b):
    return jnp.dot(a, b, preferred_element_type=F32)


def split(a):
    high = a.astype(BF16)
    return high, (a - high.astype(F32)).astype(BF16)


def product(a, b):
    return dot(a[0], b[0]) + (dot(a[1], b[0]) + dot(a[0], b[1]))


def corner(left, middle, right):
    return -product(split(product(left, split(middle))), right)


def invert_tile(tile):
    size = tile.shape[0]
    down = lax.broadcasted_iota(jnp.int32, tile.shape, 0)
    across = lax.broadcasted_iota(jnp.int32, tile.shape, 1)
    span = min(BASE, size)
    near = jnp.where(down // span == across // span, tile, 0.0)
    inverse = jnp.where(down == across, 1.0, 0.0) - near
    power = split(near)
    reach = 2
    while reach < span:
        power = split(product(power, power))
        inverse = inverse + product(split(inverse), power)
        reach *= 2
    while span < size:
        wide = 2 * span
        edge = jnp.where((down // wide == across // wide) & (down // span != across // span), tile, 0.0)
        parts = split(inverse)
        inverse = inverse + corner(parts, edge, parts)
        span = wide
    return inverse


def invert(factor_t, pivot_row, high_ref, low_ref):
    width = factor_t.shape[0]
    down = lax.broadcasted_iota(jnp.int32, (width, width), 0)
    across = lax.broadcasted_iota(jnp.int32, (width, width), 1)
    unit = jnp.where(across > down, factor_t, 0.0) / pivot_row
    size = min(LANES, width)
    blocks = [invert_tile(unit[at : at + size, at : at + size]) for at in range(0, width, size)]
    while size < width:
        joined = []
        for index in range(0, len(blocks), 2):
            at = index * size
            first, second = blocks[index], blocks[index + 1]
            edge = corner(split(first), unit[at : at + size, at + size : at + 2 * size], split(second))
            top = jnp.concatenate([first, edge], axis=1)
            bottom = jnp.concatenate([jnp.zeros_like(first), second], axis=1)
            joined.append(jnp.concatenate([top, bottom], axis=0))
        blocks = joined
        size *= 2
    high, low = split(blocks[0])
    high_ref[...] = high
    low_ref[...] = low


def kernel(
    n_row, n_rhs, parts,
    factor_ref, pivot_ref, right_ref, out_ref,
    panels, solved, work, high_ref, low_ref,
    far_send, far_recv, near_send, near_recv, x_send, x_recv,
):
    count, rows, slab = factor_ref.shape
    n_chip = n_rhs // CORES
    bits = [b for b in range(n_row.bit_length()) if 2**b < n_row]
    piece = right_ref.shape[1] // parts
    row, col = lax.axis_index("row"), lax.axis_index("rhs")
    chip, core = col // CORES, col % CORES
    sibling = col + 1 - 2 * core

    def flip(b):
        return row + (1 - 2 * ((row // 2**b) % 2)) * 2**b

    def peer(d):
        return lax.rem(chip + d, n_chip) * CORES + core

    barrier = pltpu.get_barrier_semaphore()
    partners = [{"rhs": peer(d)} for d in range(1, n_chip)] + [{"rhs": sibling}] + [{"row": flip(b)} for b in bits]
    for partner in partners:
        pl.semaphore_signal(barrier, inc=1, device_id=partner, device_id_type=pl.DeviceIdType.MESH)

    def place(owner):
        return pl.ds(pl.multiple_of(owner * slab, slab), slab)

    for k in range(count):
        panels[k, place(col), :] = factor_ref[k].astype(F32).T.astype(panels.dtype)
    pl.semaphore_wait(barrier, len(partners))

    def remote(src, dst, send, recv, target):
        return pltpu.make_async_remote_copy(
            src_ref=src, dst_ref=dst, send_sem=send, recv_sem=recv, device_id=target, device_id_type=pl.DeviceIdType.MESH
        )

    def far(k, d):
        ref = panels.at[k, place(col), :]
        return remote(ref, ref, far_send.at[k, d], far_recv.at[k, d], {"rhs": peer(d)})

    def near(k, d):
        ref = panels.at[k, place(lax.rem(chip + n_chip - d, n_chip) * CORES + core), :]
        return remote(ref, ref, near_send.at[k, d], near_recv.at[k, d], {"rhs": sibling})

    for k in range(count):

        @pl.when(row >= k)
        def _():
            for d in range(1, n_chip):
                far(k, d).start()
            near(k, 0).start()

    work[...] = right_ref[...].T

    for k in range(count):

        @pl.when(row >= k)
        def _():
            for d in range(1, n_chip):
                far(k, d).wait_recv()
                near(k, d).start()

    for k in range(count):

        @pl.when(row >= k)
        def _():
            for d in range(n_chip):
                near(k, d).wait_recv()

    @pl.when(row < count)
    def _():
        invert(panels[row].astype(F32), pivot_ref[pl.ds(row, 1), :], high_ref, low_ref)

    def part_rows(p):
        return pl.ds(p * piece, piece)

    def send(k, p, b):
        ref = solved.at[k, :, part_rows(p), :]
        return remote(ref, ref, x_send.at[k, p, b], x_recv.at[k, p], {"row": flip(b)})

    def takes(k, b):
        go = row >= 0
        for low in range(b + 1):
            go = jnp.logical_and(go, (row // 2**low) % 2 == (k // 2**low) % 2)
        if b == 0:
            go = jnp.logical_and(go, flip(b) > k)
        return go

    def pass_on(k, p):
        for b in reversed(bits):

            @pl.when(takes(k, b))
            def _():
                send(k, p, b).start()

    def step(k, p):
        at = part_rows(p)

        @pl.when(row == k)
        def _():
            right = split(work[at, :] / pivot_ref[k : k + 1, :])
            x = product(right, (high_ref[...], low_ref[...]))
            work[at, :] = x
            solved[k, 0, at, :], solved[k, 1, at, :] = split(x)
            pass_on(k, p)

        leaf = (row // 1) % 2 != k % 2

        @pl.when(jnp.logical_or(row > k, jnp.logical_and(row < k, jnp.logical_not(leaf))))
        def _():
            send(k, p, 0).wait_recv()
            pass_on(k, p)

        @pl.when(row > k)
        def _():
            panel = panels[k].astype(BF16)
            work[at, :] -= dot(solved[k, 0, at, :], panel) + dot(solved[k, 1, at, :], panel)

    @pl.when(row < count)
    def _():
        for p in range(parts):
            for k in range(count):
                step(k, p)

    @pl.when(row >= count)
    def _():
        for k in range(count):
            for p in range(parts):
                step(k, p)

    out_ref[...] = work[...].T

    for k in range(count):

        @pl.when(row >= k)
        def _():
            for d in range(1, n_chip):
                far(k, d).wait_send()
            for d in range(n_chip):
                near(k, d).wait_send()

        for b in bits:

            @pl.when(takes(k, b))
            def _():
                for p in range(parts):
                    send(k, p, b).wait_send()


def body(n_row, n_rhs, factor, pivots, right_sides):
    count, rows, slab = factor.shape
    width = pivots.shape[1]
    columns = right_sides.shape[1]
    assert rows == width and n_rhs % CORES == 0
    parts = 2
    n_chip = n_rhs // CORES
    n_bits = max(1, (n_row - 1).bit_length())
    wire = BF16 if slab % 16 == 0 else F32
    vmem = pl.BlockSpec(memory_space=pltpu.VMEM)
    dma = pltpu.SemaphoreType.DMA
    return pl.pallas_call(
        functools.partial(kernel, n_row, n_rhs, parts),
        out_shape=jax.ShapeDtypeStruct(right_sides.shape, F32),
        in_specs=[vmem] * 3,
        out_specs=vmem,
        scratch_shapes=[
            pltpu.VMEM((count, width, rows), wire),
            pltpu.VMEM((count, 2, columns, width), BF16),
            pltpu.VMEM((columns, rows), F32),
            pltpu.VMEM((width, width), BF16),
            pltpu.VMEM((width, width), BF16),
            dma((count, n_chip)),
            dma((count, n_chip)),
            dma((count, n_chip)),
            dma((count, n_chip)),
            dma((count, parts, n_bits)),
            dma((count, parts)),
        ],
        compiler_params=pltpu.CompilerParams(collective_id=0, has_side_effects=True, vmem_limit_bytes=40 * 2**20),
    )(factor, pivots, right_sides)


def solution(mesh):
    in_specs = (P(None, "row", "rhs"), P(), P("row", "rhs"))
    out_specs = P("row", "rhs")
    part = functools.partial(body, mesh.shape["row"], mesh.shape["rhs"])
    return jax.shard_map(part, mesh=mesh, in_specs=in_specs, out_specs=out_specs, check_vma=False)
```

time: 200 us -> 39.5 us (0.20); the launches traced: 198 us -> 39.4 us
  other arithmetic: 81.9 us -> 0 us
  waiting for transfers between devices: 65.9 us -> 0 us
  Pallas kernels: 0 us -> 37.5 us
  local copies, waits for them, and re-layouts: 27.6 us -> 1.83 us
  between operations: 13.4 us -> 0.03 us
  matrix products: 8.71 us -> 0 us
    another operation x4 -> x0, other arithmetic: 80.5 us -> none  [solve_block(): lax.linalg.triangular_solve(diag_k, resid_rows, left_side=True, lower=True)]
    psum x2 -> x0, waiting for transfers between devices: 42.6 us -> none  [broadcast(): return lax.psum(kept, axis)]
    pallas_call x0 -> x1, Pallas kernels: none -> 37.5 us  [body(): pl.pallas_call(functools.partial(kernel, n_row, n_rhs, parts), out_shape=...]
    all_gather x1 -> x0, waiting for transfers between devices: 23.3 us -> none  [body(): every_panel = lax.all_gather(factor, 'rhs', axis=2, tiled=True)]
    another operation x27 -> x0, local copies, waits for them, and re-layouts: 19.4 us -> none  [solve_block(): lax.linalg.triangular_solve(diag_k, resid_rows, left_side=True, lower=True)]
    another operation x14 -> x0, matrix products: 4.75 us -> none  [solve_block(): lax.linalg.triangular_solve(diag_k, resid_rows, left_side=True, lower=True)]
    dot_general x2 -> x0, matrix products: 3.96 us -> none  [advance(): jnp.dot(panel.astype(jnp.float32), solved_rows, precision=lax.Precision.H...]
    slice x2 -> x0, local copies, waits for them, and re-layouts: 3.28 us -> none  [the longest x1 3.27 us: body(): panel = every_panel[index]]
  transfers between devices with their start and end apart: 3 -> 0, of which waited for: 2 -> 0; matrix products, arithmetic and copies ran while one was open for 24% -> 0% of each run, Pallas kernels for 0% -> 0%
where the time goes in v1:
time: 39.5 us; the launch traced here: 39.4 us
  Pallas kernels  37.5 us (95%)
  local copies, waits for them, and re-layouts  1.83 us (5%)
    pallas_call x1, Pallas kernels, body(): pl.pallas_call(functools.partial(kernel, n_row, n_rhs, parts), out_shape=...  37.5 us
    unnamed x6, local copies, waits for them, and re-layouts  1.83 us

profile of v1, /device:TPU:4, one launch (start us, length us, event | category | flops | bytes accessed | tf_op | source)
XLA Modules:
  0.0 39.4 jit_solution(7617749897329642880)
XLA Ops:
  0.0 0.0 copy-start
  0.0 0.0 copy-start.1
  0.0 1.1 %copy.4.factor_ref = bf16[2,512,64]{2,1,0:T(8,128)(2,1)S(1)} copy(bf16[2,512,64]{1,2,0:T(8,128)(2,1)} %param.3) | data formatting | bytes 262144 | tf_op args[0]
  1.1 0.0 copy-done
  1.1 0.0 copy-done.1
  1.2 37.5 %shard_map.37 = f32[512,128]{1,0:T(8,128)S(1)} custom-call(bf16[2,512,64]{2,1,0:T(8,128)(2,1)S(1)} %copy.4.factor_ref, f32[2,512]{1,0:T(2,128)S(1)} %copy-done.1, f32[512,128]{1,0:T(8,128)S(1)} %copy-done), custom_call_target="tpu_custom_call" | custom-call | tf_op jit(solution)/shard_map/pallas_call | solution.py:240
  38.7 0.7 %copy.6 = f32[512,128]{1,0:T(8,128)} copy(f32[512,128]{1,0:T(8,128)S(1)} %shard_map.37) | data formatting | bytes 524288
Async XLA Ops:
  0.0 1.1 %copy-start = (f32[512,128]{1,0:T(8,128)S(1)}, f32[512,128]{1,0:T(8,128)}, u32[]{:S(2)}) copy-start(f32[512,128]{1,0:T(8,128)} %right_ref.1) | copy-start | bytes 786436
  0.0 1.1 %copy-start.1 = (f32[2,512]{1,0:T(2,128)S(1)}, f32[2,512]{1,0:T(2,128)}, u32[]{:S(2)}) copy-start(f32[2,512]{1,0:T(2,128)} %pivot_ref.1) | copy-start | bytes 12292

commit v2 on v1

--- a/solution.py
+++ b/solution.py
@@ -28,7 +28,8 @@
 
 
 def corner(left, middle, right):
-    return -product(split(product(left, split(middle))), right)
+    inner = dot(left[0], middle) + dot(left[1], middle)
+    return split(-product(split(inner), right))
 
 
 def invert_tile(tile):
@@ -48,42 +49,50 @@
         wide = 2 * span
         edge = jnp.where((down // wide == across // wide) & (down // span != across // span), tile, 0.0)
         parts = split(inverse)
-        inverse = inverse + corner(parts, edge, parts)
+        inverse = inverse - product(split(product(parts, split(edge))), parts)
         span = wide
     return inverse
 
 
-def invert(factor_t, pivot_row, high_ref, low_ref):
-    width = factor_t.shape[0]
-    down = lax.broadcasted_iota(jnp.int32, (width, width), 0)
-    across = lax.broadcasted_iota(jnp.int32, (width, width), 1)
-    unit = jnp.where(across > down, factor_t, 0.0) / pivot_row
-    size = min(LANES, width)
-    blocks = [invert_tile(unit[at : at + size, at : at + size]) for at in range(0, width, size)]
+def diagonal(tile, pivot_row):
+    down = lax.broadcasted_iota(jnp.int32, tile.shape, 0)
+    across = lax.broadcasted_iota(jnp.int32, tile.shape, 1)
+    pivot_column = jnp.sum(jnp.where(down == across, pivot_row, 0.0), axis=1, keepdims=True)
+    unit = jnp.where(across > down, tile.astype(F32), 0.0) / pivot_row
+    return split(invert_tile(unit) / pivot_column)
+
+
+def combine(blocks, panel, out_ref):
+    width = panel.shape[0]
+    size = width // len(blocks)
     while size < width:
         joined = []
         for index in range(0, len(blocks), 2):
             at = index * size
             first, second = blocks[index], blocks[index + 1]
-            edge = corner(split(first), unit[at : at + size, at + size : at + 2 * size], split(second))
-            top = jnp.concatenate([first, edge], axis=1)
-            bottom = jnp.concatenate([jnp.zeros_like(first), second], axis=1)
-            joined.append(jnp.concatenate([top, bottom], axis=0))
+            edge = corner(first, panel[at : at + size, at + size : at + 2 * size].astype(BF16), second)
+            block = []
+            for one, other, between in zip(first, second, edge):
+                top = jnp.concatenate([one, between], axis=1)
+                bottom = jnp.concatenate([jnp.zeros_like(one), other], axis=1)
+                block.append(jnp.concatenate([top, bottom], axis=0))
+            joined.append(block)
         blocks = joined
         size *= 2
-    high, low = split(blocks[0])
-    high_ref[...] = high
-    low_ref[...] = low
+    out_ref[0], out_ref[1] = blocks[0]
 
 
 def kernel(
     n_row, n_rhs, parts,
     factor_ref, pivot_ref, right_ref, out_ref,
-    panels, solved, work, high_ref, low_ref,
-    far_send, far_recv, near_send, near_recv, x_send, x_recv,
+    panels, solved, work, inverse, tiles,
+    far_send, far_recv, near_send, near_recv, tile_send, tile_recv, tile_near_send, tile_near_recv, x_send, x_recv,
 ):
-    count, rows, slab = factor_ref.shape
+    count, slab, rows = factor_ref.shape
+    width = pivot_ref.shape[1]
     n_chip = n_rhs // CORES
+    size = tiles.shape[-1]
+    spread = CORES * slab == size
     bits = [b for b in range(n_row.bit_length()) if 2**b < n_row]
     piece = right_ref.shape[1] // parts
     row, col = lax.axis_index("row"), lax.axis_index("rhs")
@@ -105,7 +114,7 @@
         return pl.ds(pl.multiple_of(owner * slab, slab), slab)
 
     for k in range(count):
-        panels[k, place(col), :] = factor_ref[k].astype(F32).T.astype(panels.dtype)
+        panels[k, place(col), :] = factor_ref[k].astype(panels.dtype)
     pl.semaphore_wait(barrier, len(partners))
 
     def remote(src, dst, send, recv, target):
@@ -121,34 +130,94 @@
         ref = panels.at[k, place(lax.rem(chip + n_chip - d, n_chip) * CORES + core), :]
         return remote(ref, ref, near_send.at[k, d], near_recv.at[k, d], {"rhs": sibling})
 
-    for k in range(count):
-
-        @pl.when(row >= k)
-        def _():
+    def row_pivots(at):
+        return sum(jnp.where(row == k, pivot_ref[k : k + 1, at : at + size], 0.0) for k in range(count))
+
+    def own_pivots():
+        return sum(jnp.where(chip == at // size, row_pivots(at), 0.0) for at in range(0, width, size))
+
+    def far_tile(d):
+        ref = tiles.at[chip, :, place_half(), :]
+        return remote(ref, ref, tile_send.at[d], tile_recv.at[d], {"rhs": peer(d)})
+
+    def near_tile(d):
+        ref = tiles.at[lax.rem(chip + n_chip - d, n_chip), :, place_half(), :]
+        return remote(ref, ref, tile_near_send.at[d], tile_near_recv.at[d], {"rhs": sibling})
+
+    def place_half():
+        return pl.ds(pl.multiple_of(core * (size // CORES), size // CORES), size // CORES)
+
+    def launch(k):
+        for d in range(1, n_chip):
+            far(k, d).start()
+        near(k, 0).start()
+
+    @pl.when(row < count)
+    def _():
+        launch(row)
+
+    for k in range(count):
+
+        @pl.when(row > k)
+        def _():
+            launch(k)
+
+    work[...] = right_ref[...].T
+
+    if spread:
+
+        @pl.when(row < count)
+        def _():
+            near(row, 0).wait_recv()
+            at = pl.ds(pl.multiple_of(chip * size, size), size)
+            tiles[chip, 0], tiles[chip, 1] = diagonal(panels[row, at, at], own_pivots())
             for d in range(1, n_chip):
-                far(k, d).start()
-            near(k, 0).start()
-
-    work[...] = right_ref[...].T
-
-    for k in range(count):
-
-        @pl.when(row >= k)
-        def _():
+                far_tile(d).start()
+
+    def relay(k):
+        for d in range(1, n_chip):
+            far(k, d).wait_recv()
+            near(k, d).start()
+
+    def settle(k, first):
+        for d in range(first, n_chip):
+            near(k, d).wait_recv()
+
+    @pl.when(row < count)
+    def _():
+        relay(row)
+
+    for k in range(count):
+
+        @pl.when(row > k)
+        def _():
+            relay(k)
+
+    @pl.when(row < count)
+    def _():
+        if spread:
             for d in range(1, n_chip):
-                far(k, d).wait_recv()
-                near(k, d).start()
-
-    for k in range(count):
-
-        @pl.when(row >= k)
-        def _():
-            for d in range(n_chip):
-                near(k, d).wait_recv()
-
-    @pl.when(row < count)
-    def _():
-        invert(panels[row].astype(F32), pivot_ref[pl.ds(row, 1), :], high_ref, low_ref)
+                far_tile(d).wait_recv()
+                near_tile(d).start()
+            settle(row, 1)
+            for d in range(1, n_chip):
+                near_tile(d).wait_recv()
+            panel = panels[row]
+            blocks = [(tiles[at, 0], tiles[at, 1]) for at in range(n_chip)]
+        else:
+            settle(row, 0)
+            panel = panels[row]
+            blocks = []
+            for at in range(0, width, size):
+                whole = slice(at, at + size)
+                blocks.append(diagonal(panel[whole, whole], row_pivots(at)))
+        combine(blocks, panel, inverse)
+
+    for k in range(count):
+
+        @pl.when(row > k)
+        def _():
+            settle(k, 0)
 
     def part_rows(p):
         return pl.ds(p * piece, piece)
@@ -177,8 +246,7 @@
 
         @pl.when(row == k)
         def _():
-            right = split(work[at, :] / pivot_ref[k : k + 1, :])
-            x = product(right, (high_ref[...], low_ref[...]))
+            x = product(split(work[at, :]), (inverse[0], inverse[1]))
             work[at, :] = x
             solved[k, 0, at, :], solved[k, 1, at, :] = split(x)
             pass_on(k, p)
@@ -218,6 +286,14 @@
             for d in range(n_chip):
                 near(k, d).wait_send()
 
+        if spread:
+
+            @pl.when(row == k)
+            def _():
+                for d in range(1, n_chip):
+                    far_tile(d).wait_send()
+                    near_tile(d).wait_send()
+
         for b in bits:
 
             @pl.when(takes(k, b))
@@ -227,14 +303,16 @@
 
 
 def body(n_row, n_rhs, factor, pivots, right_sides):
-    count, rows, slab = factor.shape
+    factor = jnp.swapaxes(factor, 1, 2)
+    count, slab, rows = factor.shape
     width = pivots.shape[1]
     columns = right_sides.shape[1]
     assert rows == width and n_rhs % CORES == 0
-    parts = 2
+    parts = 4 if columns % 64 == 0 else 1
     n_chip = n_rhs // CORES
     n_bits = max(1, (n_row - 1).bit_length())
     wire = BF16 if slab % 16 == 0 else F32
+    tile = min(LANES, width)
     vmem = pl.BlockSpec(memory_space=pltpu.VMEM)
     dma = pltpu.SemaphoreType.DMA
     return pl.pallas_call(
@@ -246,12 +324,16 @@
             pltpu.VMEM((count, width, rows), wire),
             pltpu.VMEM((count, 2, columns, width), BF16),
             pltpu.VMEM((columns, rows), F32),
-            pltpu.VMEM((width, width), BF16),
-            pltpu.VMEM((width, width), BF16),
+            pltpu.VMEM((2, width, width), BF16),
+            pltpu.VMEM((width // tile, 2, tile, tile), BF16),
             dma((count, n_chip)),
             dma((count, n_chip)),
             dma((count, n_chip)),
             dma((count, n_chip)),
+            dma((n_chip,)),
+            dma((n_chip,)),
+            dma((n_chip,)),
+            dma((n_chip,)),
             dma((count, parts, n_bits)),
             dma((count, parts)),
         ],

time: 39.5 us -> 37.4 us (0.947)
  Pallas kernels: 37.5 us -> 34 us
  local copies, waits for them, and re-layouts: 1.83 us -> 3.24 us
    pallas_call x1, Pallas kernels: 37.5 us -> 34 us  [body(): pl.pallas_call(functools.partial(kernel, n_row, n_rhs, parts), out_shape=...]
    unnamed x6 -> x7, local copies, waits for them, and re-layouts: 1.83 us -> 3.24 us
where the time goes in v2:
time: 37.4 us; the launch traced here: 37.2 us
  Pallas kernels  34 us (91%)
  local copies, waits for them, and re-layouts  3.24 us (9%)
    pallas_call x1, Pallas kernels, body(): pl.pallas_call(functools.partial(kernel, n_row, n_rhs, parts), out_shape=...  34 us
    unnamed x7, local copies, waits for them, and re-layouts  3.24 us

profile of v2, /device:TPU:4, one launch (start us, length us, event | category | flops | bytes accessed | tf_op | source)
XLA Modules:
  0.0 37.2 jit_solution(21344051303764383)
XLA Ops:
  0.0 0.0 copy-start
  0.0 0.9 %copy-done = f32[512,128]{1,0:T(8,128)S(1)} copy-done((f32[512,128]{1,0:T(8,128)S(1)}, f32[512,128]{1,0:T(8,128)}, u32[]{:S(2)}) %copy-start) | copy-done | bytes 262168
  1.0 0.0 copy-start.1
  1.0 0.9 %copy-done.1 = bf16[2,512,64]{1,2,0:T(8,128)(2,1)S(1)} copy-done((bf16[2,512,64]{1,2,0:T(8,128)(2,1)S(1)}, bf16[2,512,64]{1,2,0:T(8,128)(2,1)}, u32[]{:S(2)}) %copy-start.1) | copy-done | bytes 131096
  1.9 0.0 copy-start.2
  1.9 0.7 %copy-done.2 = f32[2,512]{1,0:T(2,128)S(1)} copy-done((f32[2,512]{1,0:T(2,128)S(1)}, f32[2,512]{1,0:T(2,128)}, u32[]{:S(2)}) %copy-start.2) | copy-done | bytes 4120
  2.5 34.0 %shard_map.37 = f32[512,128]{1,0:T(8,128)S(1)} custom-call(bf16[2,64,512]{2,1,0:T(8,128)(2,1)S(1)} %bitcast.1, f32[2,512]{1,0:T(2,128)S(1)} %copy-done.2, f32[512,128]{1,0:T(8,128)S(1)} %copy-done), custom_call_target="tpu_custom_call" | custom-call | tf_op jit(solution)/shard_map/pallas_call | solution.py:318
  36.5 0.7 %copy.5 = f32[512,128]{1,0:T(8,128)} copy(f32[512,128]{1,0:T(8,128)S(1)} %shard_map.37) | data formatting | bytes 524288
Async XLA Ops:
  0.0 0.9 %copy-start = (f32[512,128]{1,0:T(8,128)S(1)}, f32[512,128]{1,0:T(8,128)}, u32[]{:S(2)}) copy-start(f32[512,128]{1,0:T(8,128)} %right_ref.1) | copy-start | bytes 786436
  1.0 0.9 %copy-start.1 = (bf16[2,512,64]{1,2,0:T(8,128)(2,1)S(1)}, bf16[2,512,64]{1,2,0:T(8,128)(2,1)}, u32[]{:S(2)}) copy-start(bf16[2,512,64]{1,2,0:T(8,128)(2,1)} %param.3) | copy-start | bytes 393220
  1.9 0.7 %copy-start.2 = (f32[2,512]{1,0:T(2,128)S(1)}, f32[2,512]{1,0:T(2,128)}, u32[]{:S(2)}) copy-start(f32[2,512]{1,0:T(2,128)} %pivot_ref.1) | copy-start | bytes 12292

commit v3 on v2

--- a/solution.py
+++ b/solution.py
@@ -24,12 +24,17 @@
 
 
 def product(a, b):
-    return dot(a[0], b[0]) + (dot(a[1], b[0]) + dot(a[0], b[1]))
+    return dot_rows(a, b[0]) + dot(a[0], b[1])
+
+
+def dot_rows(a, b):
+    size = a[0].shape[0]
+    both = dot(jnp.concatenate([a[0], a[1]], axis=0), b)
+    return both[:size] + both[size:]
 
 
 def corner(left, middle, right):
-    inner = dot(left[0], middle) + dot(left[1], middle)
-    return split(-product(split(inner), right))
+    return split(-product(split(dot_rows(left, middle)), right))
 
 
 def invert_tile(tile):
@@ -84,8 +89,9 @@
 
 def kernel(
     n_row, n_rhs, parts,
-    factor_ref, pivot_ref, right_ref, out_ref,
-    panels, solved, work, inverse, tiles,
+    factor_hbm, pivot_hbm, right_hbm, out_ref,
+    panels, solved, work, inverse, tiles, merged, factor_ref, pivot_ref, right_ref,
+    fetch,
     far_send, far_recv, near_send, near_recv, tile_send, tile_recv, tile_near_send, tile_near_recv, x_send, x_recv,
 ):
     count, slab, rows = factor_ref.shape
@@ -95,6 +101,7 @@
     spread = CORES * slab == size
     bits = [b for b in range(n_row.bit_length()) if 2**b < n_row]
     piece = right_ref.shape[1] // parts
+    direct = panels.dtype == factor_hbm.dtype
     row, col = lax.axis_index("row"), lax.axis_index("rhs")
     chip, core = col // CORES, col % CORES
     sibling = col + 1 - 2 * core
@@ -113,8 +120,21 @@
     def place(owner):
         return pl.ds(pl.multiple_of(owner * slab, slab), slab)
 
-    for k in range(count):
-        panels[k, place(col), :] = factor_ref[k].astype(panels.dtype)
+    def fetched(index, src, dst):
+        return pltpu.make_async_copy(src, dst, fetch.at[index])
+
+    in_right = fetched(0, right_hbm, right_ref)
+    in_pivot = fetched(1, pivot_hbm, pivot_ref)
+    if direct:
+        in_factor = [fetched(2 + k, factor_hbm.at[k], panels.at[k, place(col), :]) for k in range(count)]
+    else:
+        in_factor = [fetched(2 + k, factor_hbm.at[k], factor_ref.at[k]) for k in range(count)]
+    for copy in in_factor + [in_right, in_pivot]:
+        copy.start()
+    if not direct:
+        for k in range(count):
+            in_factor[k].wait()
+            panels[k, place(col), :] = factor_ref[k].astype(panels.dtype)
     pl.semaphore_wait(barrier, len(partners))
 
     def remote(src, dst, send, recv, target):
@@ -124,11 +144,11 @@
 
     def far(k, d):
         ref = panels.at[k, place(col), :]
-        return remote(ref, ref, far_send.at[k, d], far_recv.at[k, d], {"rhs": peer(d)})
+        return remote(factor_hbm.at[k] if direct else ref, ref, far_send.at[k, d], far_recv.at[k, d], {"rhs": peer(d)})
 
     def near(k, d):
         ref = panels.at[k, place(lax.rem(chip + n_chip - d, n_chip) * CORES + core), :]
-        return remote(ref, ref, near_send.at[k, d], near_recv.at[k, d], {"rhs": sibling})
+        return remote(factor_hbm.at[k] if direct and d == 0 else ref, ref, near_send.at[k, d], near_recv.at[k, d], {"rhs": sibling})
 
     def row_pivots(at):
         return sum(jnp.where(row == k, pivot_ref[k : k + 1, at : at + size], 0.0) for k in range(count))
@@ -162,6 +182,11 @@
         def _():
             launch(k)
 
+    if direct:
+        for copy in in_factor:
+            copy.wait()
+    in_right.wait()
+    in_pivot.wait()
     work[...] = right_ref[...].T
 
     if spread:
@@ -186,15 +211,6 @@
     @pl.when(row < count)
     def _():
         relay(row)
-
-    for k in range(count):
-
-        @pl.when(row > k)
-        def _():
-            relay(k)
-
-    @pl.when(row < count)
-    def _():
         if spread:
             for d in range(1, n_chip):
                 far_tile(d).wait_recv()
@@ -212,12 +228,24 @@
                 whole = slice(at, at + size)
                 blocks.append(diagonal(panel[whole, whole], row_pivots(at)))
         combine(blocks, panel, inverse)
+        work[...] = product(split(work[...]), (inverse[0], inverse[1]))
 
     for k in range(count):
 
         @pl.when(row > k)
         def _():
+            relay(k)
+
+    for k in range(count):
+
+        @pl.when(row > k)
+        def _():
             settle(k, 0)
+
+        @pl.when(jnp.logical_and(row > k, row < count))
+        def _():
+            panel = panels[k].astype(BF16)
+            merged[k, 0], merged[k, 1] = split(dot(panel, inverse[0]) + dot(panel, inverse[1]))
 
     def part_rows(p):
         return pl.ds(p * piece, piece)
@@ -246,9 +274,7 @@
 
         @pl.when(row == k)
         def _():
-            x = product(split(work[at, :]), (inverse[0], inverse[1]))
-            work[at, :] = x
-            solved[k, 0, at, :], solved[k, 1, at, :] = split(x)
+            solved[k, 0, at, :], solved[k, 1, at, :] = split(work[at, :])
             pass_on(k, p)
 
         leaf = (row // 1) % 2 != k % 2
@@ -258,10 +284,13 @@
             send(k, p, 0).wait_recv()
             pass_on(k, p)
 
-        @pl.when(row > k)
-        def _():
-            panel = panels[k].astype(BF16)
-            work[at, :] -= dot(solved[k, 0, at, :], panel) + dot(solved[k, 1, at, :], panel)
+        @pl.when(jnp.logical_and(row > k, row < count))
+        def _():
+            work[at, :] -= product((solved[k, 0, at, :], solved[k, 1, at, :]), (merged[k, 0], merged[k, 1]))
+
+        @pl.when(row >= count)
+        def _():
+            work[at, :] -= dot_rows((solved[k, 0, at, :], solved[k, 1, at, :]), panels[k].astype(BF16))
 
     @pl.when(row < count)
     def _():
@@ -318,7 +347,7 @@
     return pl.pallas_call(
         functools.partial(kernel, n_row, n_rhs, parts),
         out_shape=jax.ShapeDtypeStruct(right_sides.shape, F32),
-        in_specs=[vmem] * 3,
+        in_specs=[pl.BlockSpec(memory_space=pl.ANY)] * 3,
         out_specs=vmem,
         scratch_shapes=[
             pltpu.VMEM((count, width, rows), wire),
@@ -326,6 +355,11 @@
             pltpu.VMEM((columns, rows), F32),
             pltpu.VMEM((2, width, width), BF16),
             pltpu.VMEM((width // tile, 2, tile, tile), BF16),
+            pltpu.VMEM((count, 2, width, width), BF16),
+            pltpu.VMEM(factor.shape, factor.dtype),
+            pltpu.VMEM(pivots.shape, F32),
+            pltpu.VMEM(right_sides.shape, F32),
+            dma((count + 2,)),
             dma((count, n_chip)),
             dma((count, n_chip)),
             dma((count, n_chip)),
@@ -337,7 +371,7 @@
             dma((count, parts, n_bits)),
             dma((count, parts)),
         ],
-        compiler_params=pltpu.CompilerParams(collective_id=0, has_side_effects=True, vmem_limit_bytes=40 * 2**20),
+        compiler_params=pltpu.CompilerParams(collective_id=0, has_side_effects=True, vmem_limit_bytes=56 * 2**20),
     )(factor, pivots, right_sides)
 
 

time: 37.4 us -> 36.6 us (0.979)
  local copies, waits for them, and re-layouts: 3.24 us -> 1.67 us
  Pallas kernels: 34 us -> 34.8 us
    unnamed x7 -> x1, local copies, waits for them, and re-layouts: 3.24 us -> 1.67 us
    pallas_call x1, Pallas kernels: 34 us -> 34.8 us  [body(): pl.pallas_call(functools.partial(kernel, n_row, n_rhs, parts), out_shape=...]
where the time goes in v3:
time: 36.6 us; the launch traced here: 36.5 us
  Pallas kernels  34.8 us (95%)
  local copies, waits for them, and re-layouts  1.67 us (5%)
    pallas_call x1, Pallas kernels, body(): pl.pallas_call(functools.partial(kernel, n_row, n_rhs, parts), out_shape=...  34.8 us
    unnamed x1, local copies, waits for them, and re-layouts  1.67 us

profile of v3, /device:TPU:4, one launch (start us, length us, event | category | flops | bytes accessed | tf_op | source)
XLA Modules:
  0.0 36.5 jit_solution(4556506145639636588)
XLA Ops:
  0.0 34.8 %shard_map.37 = f32[512,128]{1,0:T(8,128)} custom-call(bf16[2,64,512]{2,1,0:T(8,128)(2,1)} %bitcast.1, f32[2,512]{1,0:T(2,128)} %pivot_hbm.1, f32[512,128]{1,0:T(8,128)} %right_hbm.1), custom_call_target="tpu_custom_call" | custom-call | tf_op jit(solution)/shard_map/pallas_call | solution.py:347
  34.8 1.7 %copy.5 = f32[512,128]{1,0:T(8,128)} copy(f32[512,128]{1,0:T(8,128)} %shard_map.37) | data formatting | bytes 524288

commit v4 on v3

--- a/solution.py
+++ b/solution.py
@@ -67,15 +67,14 @@
     return split(invert_tile(unit) / pivot_column)
 
 
-def combine(blocks, panel, out_ref):
-    width = panel.shape[0]
+def combine(blocks, width, panel, out_ref):
     size = width // len(blocks)
     while size < width:
         joined = []
         for index in range(0, len(blocks), 2):
             at = index * size
             first, second = blocks[index], blocks[index + 1]
-            edge = corner(first, panel[at : at + size, at + size : at + 2 * size].astype(BF16), second)
+            edge = corner(first, panel(slice(at, at + size), slice(at + size, at + 2 * size)), second)
             block = []
             for one, other, between in zip(first, second, edge):
                 top = jnp.concatenate([one, between], axis=1)
@@ -167,6 +166,68 @@
     def place_half():
         return pl.ds(pl.multiple_of(core * (size // CORES), size // CORES), size // CORES)
 
+    def source(d):
+        return lax.rem(chip + n_chip - d, n_chip)
+
+    def beyond(c):
+        return pl.ds(size * (c + 1), width - size * (c + 1))
+
+    def far_own(c, d):
+        src = factor_hbm.at[row, :, beyond(c)] if direct else panels.at[row, place(col), beyond(c)]
+        dst = panels.at[row, place(col), beyond(c)]
+        return remote(src, dst, far_send.at[row, d], far_recv.at[row, d], {"rhs": peer(d)})
+
+    def near_own(c, d):
+        ref = panels.at[row, place(c * CORES + core), beyond(c)]
+        return remote(ref, ref, near_send.at[row, d], near_recv.at[row, d], {"rhs": sibling})
+
+    def each_source(act):
+        for d in range(1, n_chip):
+            for c in range(n_chip - 1):
+
+                @pl.when(source(d) == c)
+                def _():
+                    act(c, d)
+
+    def launch_own():
+        near(row, 0).start()
+        if not spread:
+            for d in range(1, n_chip):
+                far(row, d).start()
+            return
+        for c in range(n_chip - 1):
+
+            @pl.when(chip == c)
+            def _():
+                for d in range(1, n_chip):
+                    far_own(c, d).start()
+
+    def relay_own():
+        if not spread:
+            return relay(row)
+
+        def act(c, d):
+            far_own(c, d).wait_recv()
+            near_own(c, d).start()
+
+        each_source(act)
+
+    def sent_own():
+        near(row, 0).wait_send()
+        if not spread:
+            for d in range(1, n_chip):
+                far(row, d).wait_send()
+                near(row, d).wait_send()
+            return
+        for c in range(n_chip - 1):
+
+            @pl.when(chip == c)
+            def _():
+                for d in range(1, n_chip):
+                    far_own(c, d).wait_send()
+
+        each_source(lambda c, d: near_own(c, d).wait_send())
+
     def launch(k):
         for d in range(1, n_chip):
             far(k, d).start()
@@ -174,12 +235,11 @@
 
     @pl.when(row < count)
     def _():
-        launch(row)
-
-    for k in range(count):
-
-        @pl.when(row > k)
-        def _():
+        launch_own()
+
+    @pl.when(row >= count)
+    def _():
+        for k in range(count):
             launch(k)
 
     if direct:
@@ -204,30 +264,35 @@
             far(k, d).wait_recv()
             near(k, d).start()
 
-    def settle(k, first):
-        for d in range(first, n_chip):
+    def settle(k):
+        for d in range(n_chip):
             near(k, d).wait_recv()
 
     @pl.when(row < count)
     def _():
-        relay(row)
+        relay_own()
         if spread:
             for d in range(1, n_chip):
                 far_tile(d).wait_recv()
                 near_tile(d).start()
-            settle(row, 1)
+        for k in range(count - 1):
+
+            @pl.when(row > k)
+            def _():
+                launch(k)
+
+        if spread:
+            each_source(lambda c, d: near_own(c, d).wait_recv())
             for d in range(1, n_chip):
                 near_tile(d).wait_recv()
-            panel = panels[row]
             blocks = [(tiles[at, 0], tiles[at, 1]) for at in range(n_chip)]
         else:
-            settle(row, 0)
-            panel = panels[row]
+            settle(row)
             blocks = []
             for at in range(0, width, size):
                 whole = slice(at, at + size)
-                blocks.append(diagonal(panel[whole, whole], row_pivots(at)))
-        combine(blocks, panel, inverse)
+                blocks.append(diagonal(panels[row, whole, whole], row_pivots(at)))
+        combine(blocks, width, lambda down, across: panels[row, down, across].astype(BF16), inverse)
         work[...] = product(split(work[...]), (inverse[0], inverse[1]))
 
     for k in range(count):
@@ -240,7 +305,7 @@
 
         @pl.when(row > k)
         def _():
-            settle(k, 0)
+            settle(k)
 
         @pl.when(jnp.logical_and(row > k, row < count))
         def _():
@@ -308,17 +373,17 @@
 
     for k in range(count):
 
-        @pl.when(row >= k)
+        @pl.when(row > k)
         def _():
             for d in range(1, n_chip):
                 far(k, d).wait_send()
             for d in range(n_chip):
                 near(k, d).wait_send()
 
-        if spread:
-
-            @pl.when(row == k)
-            def _():
+        @pl.when(row == k)
+        def _():
+            sent_own()
+            if spread:
                 for d in range(1, n_chip):
                     far_tile(d).wait_send()
                     near_tile(d).wait_send()
@@ -347,7 +412,7 @@
     return pl.pallas_call(
         functools.partial(kernel, n_row, n_rhs, parts),
         out_shape=jax.ShapeDtypeStruct(right_sides.shape, F32),
-        in_specs=[pl.BlockSpec(memory_space=pl.ANY)] * 3,
+        in_specs=[pl.BlockSpec(memory_space=pltpu.HBM)] * 3,
         out_specs=vmem,
         scratch_shapes=[
             pltpu.VMEM((count, width, rows), wire),
@@ -371,8 +436,8 @@
             dma((count, parts, n_bits)),
             dma((count, parts)),
         ],
-        compiler_params=pltpu.CompilerParams(collective_id=0, has_side_effects=True, vmem_limit_bytes=56 * 2**20),
-    )(factor, pivots, right_sides)
+        compiler_params=pltpu.CompilerParams(collective_id=0, has_side_effects=True, vmem_limit_bytes=40 * 2**20),
+    )(*[pltpu.with_memory_space_constraint(array, pltpu.HBM) for array in (factor, pivots, right_sides)])
 
 
 def solution(mesh):

time: 36.6 us -> 33.3 us (0.910)
  Pallas kernels: 34.8 us -> 32.5 us
  local copies, waits for them, and re-layouts: 1.67 us -> 0.71 us
    pallas_call x1, Pallas kernels: 34.8 us -> 32.5 us  [body(): pl.pallas_call(functools.partial(kernel, n_row, n_rhs, parts), out_shape=...]
    unnamed x1, local copies, waits for them, and re-layouts: 1.67 us -> 0.71 us
where the time goes in v4:
time: 33.3 us; the launch traced here: 33.2 us
  Pallas kernels  32.5 us (98%)
  local copies, waits for them, and re-layouts  0.71 us (2%)
    pallas_call x1, Pallas kernels, body(): pl.pallas_call(functools.partial(kernel, n_row, n_rhs, parts), out_shape=...  32.5 us
    unnamed x1, local copies, waits for them, and re-layouts  0.71 us

profile of v4, /device:TPU:4, one launch (start us, length us, event | category | flops | bytes accessed | tf_op | source)
XLA Modules:
  0.0 33.2 jit_solution(1345713931709903824)
XLA Ops:
  0.0 32.5 %shard_map.37 = f32[512,128]{1,0:T(8,128)S(1)} custom-call(bf16[2,64,512]{2,1,0:T(8,128)(2,1)} %bitcast.1, f32[2,512]{1,0:T(2,128)} %pivot_hbm.1, f32[512,128]{1,0:T(8,128)} %right_hbm.1), custom_call_target="tpu_custom_call" | custom-call | tf_op jit(solution)/shard_map/pallas_call | solution.py:412
  32.5 0.7 %copy.5 = f32[512,128]{1,0:T(8,128)} copy(f32[512,128]{1,0:T(8,128)S(1)} %shard_map.37) | data formatting | bytes 524288

commit v5 on v4

--- a/solution.py
+++ b/solution.py
@@ -108,11 +108,16 @@
     def flip(b):
         return row + (1 - 2 * ((row // 2**b) % 2)) * 2**b
 
+    def diagonal_row():
+        return flip(0) + flip(1) - row
+
     def peer(d):
         return lax.rem(chip + d, n_chip) * CORES + core
 
     barrier = pltpu.get_barrier_semaphore()
     partners = [{"rhs": peer(d)} for d in range(1, n_chip)] + [{"rhs": sibling}] + [{"row": flip(b)} for b in bits]
+    if len(bits) > 1:
+        partners.append({"row": diagonal_row()})
     for partner in partners:
         pl.semaphore_signal(barrier, inc=1, device_id=partner, device_id_type=pl.DeviceIdType.MESH)
 
@@ -259,6 +264,14 @@
             for d in range(1, n_chip):
                 far_tile(d).start()
 
+    @pl.when(row < count)
+    def _():
+        for k in range(count - 1):
+
+            @pl.when(row > k)
+            def _():
+                launch(k)
+
     def relay(k):
         for d in range(1, n_chip):
             far(k, d).wait_recv()
@@ -275,12 +288,6 @@
             for d in range(1, n_chip):
                 far_tile(d).wait_recv()
                 near_tile(d).start()
-        for k in range(count - 1):
-
-            @pl.when(row > k)
-            def _():
-                launch(k)
-
         if spread:
             each_source(lambda c, d: near_own(c, d).wait_recv())
             for d in range(1, n_chip):
@@ -317,18 +324,28 @@
 
     def send(k, p, b):
         ref = solved.at[k, :, part_rows(p), :]
-        return remote(ref, ref, x_send.at[k, p, b], x_recv.at[k, p], {"row": flip(b)})
+        return remote(ref, ref, x_send.at[k, p, b], x_recv.at[k, p], {"row": diagonal_row() if b == len(bits) else flip(b)})
 
     def takes(k, b):
         go = row >= 0
-        for low in range(b + 1):
+        if b == len(bits):
+            if len(bits) < 2 or k < count - 1:
+                return None
+            for low in range(2):
+                go = jnp.logical_and(go, (row // 2**low) % 2 == (k // 2**low) % 2)
+            return jnp.logical_and(go, diagonal_row() > k)
+        skips = b == 0 and k == count - 1 and len(bits) > 1
+        for low in range(2 if skips else b + 1):
             go = jnp.logical_and(go, (row // 2**low) % 2 == (k // 2**low) % 2)
         if b == 0:
             go = jnp.logical_and(go, flip(b) > k)
         return go
 
+    def paths(k):
+        return [b for b in [len(bits)] + bits[::-1] if takes(k, b) is not None]
+
     def pass_on(k, p):
-        for b in reversed(bits):
+        for b in paths(k):
 
             @pl.when(takes(k, b))
             def _():
@@ -388,7 +405,7 @@
                     far_tile(d).wait_send()
                     near_tile(d).wait_send()
 
-        for b in bits:
+        for b in paths(k):
 
             @pl.when(takes(k, b))
             def _():
@@ -433,7 +450,7 @@
             dma((n_chip,)),
             dma((n_chip,)),
             dma((n_chip,)),
-            dma((count, parts, n_bits)),
+            dma((count, parts, n_bits + 1)),
             dma((count, parts)),
         ],
         compiler_params=pltpu.CompilerParams(collective_id=0, has_side_effects=True, vmem_limit_bytes=40 * 2**20),

time: 33.3 us -> 31.1 us (0.934)
  the two profiles are of different devices: /device:TPU:4 before, /device:TPU:6 now
where the time goes in v5:
time: 31.1 us; the launch traced here: 31 us
  Pallas kernels  30.2 us (97%)
  local copies, waits for them, and re-layouts  0.71 us (2%)
    pallas_call x1, Pallas kernels, body(): pl.pallas_call(functools.partial(kernel, n_row, n_rhs, parts), out_shape=...  30.2 us
    unnamed x1, local copies, waits for them, and re-layouts  0.71 us

profile of v5, /device:TPU:6, one launch (start us, length us, event | category | flops | bytes accessed | tf_op | source)
XLA Modules:
  0.0 31.0 jit_solution(1389889914369359631)
XLA Ops:
  0.0 30.2 %shard_map.37 = f32[512,128]{1,0:T(8,128)S(1)} custom-call(bf16[2,64,512]{2,1,0:T(8,128)(2,1)} %bitcast.1, f32[2,512]{1,0:T(2,128)} %pivot_hbm.1, f32[512,128]{1,0:T(8,128)} %right_hbm.1), custom_call_target="tpu_custom_call" | custom-call | tf_op jit(solution)/shard_map/pallas_call | solution.py:429
  30.2 0.7 %copy.5 = f32[512,128]{1,0:T(8,128)} copy(f32[512,128]{1,0:T(8,128)S(1)} %shard_map.37) | data formatting | bytes 524288

commit v6 on v5

--- a/solution.py
+++ b/solution.py
@@ -326,28 +326,31 @@
         ref = solved.at[k, :, part_rows(p), :]
         return remote(ref, ref, x_send.at[k, p, b], x_recv.at[k, p], {"row": diagonal_row() if b == len(bits) else flip(b)})
 
-    def takes(k, b):
+    def skips_stop(k, p):
+        return k == count - 1 and len(bits) > 1 and p >= parts // 2
+
+    def takes(k, p, b):
         go = row >= 0
         if b == len(bits):
-            if len(bits) < 2 or k < count - 1:
+            if not skips_stop(k, p):
                 return None
             for low in range(2):
                 go = jnp.logical_and(go, (row // 2**low) % 2 == (k // 2**low) % 2)
             return jnp.logical_and(go, diagonal_row() > k)
-        skips = b == 0 and k == count - 1 and len(bits) > 1
+        skips = b == 0 and skips_stop(k, p)
         for low in range(2 if skips else b + 1):
             go = jnp.logical_and(go, (row // 2**low) % 2 == (k // 2**low) % 2)
         if b == 0:
             go = jnp.logical_and(go, flip(b) > k)
         return go
 
-    def paths(k):
-        return [b for b in [len(bits)] + bits[::-1] if takes(k, b) is not None]
+    def paths(k, p):
+        return [b for b in bits + [len(bits)] if takes(k, p, b) is not None]
 
     def pass_on(k, p):
-        for b in paths(k):
-
-            @pl.when(takes(k, b))
+        for b in paths(k, p):
+
+            @pl.when(takes(k, p, b))
             def _():
                 send(k, p, b).start()
 
@@ -405,11 +408,11 @@
                     far_tile(d).wait_send()
                     near_tile(d).wait_send()
 
-        for b in paths(k):
-
-            @pl.when(takes(k, b))
-            def _():
-                for p in range(parts):
+        for p in range(parts):
+            for b in paths(k, p):
+
+                @pl.when(takes(k, p, b))
+                def _():
                     send(k, p, b).wait_send()
 
 

time: 31.1 us -> 31.6 us (1.016)
  the two profiles are of different devices: /device:TPU:6 before, /device:TPU:4 now
where the time goes in v6:
time: 31.6 us; the launch traced here: 31.4 us
  Pallas kernels  30.7 us (97%)
  local copies, waits for them, and re-layouts  0.71 us (2%)
    pallas_call x1, Pallas kernels, body(): pl.pallas_call(functools.partial(kernel, n_row, n_rhs, parts), out_shape=...  30.7 us
    unnamed x1, local copies, waits for them, and re-layouts  0.71 us

profile of v6, /device:TPU:4, one launch (start us, length us, event | category | flops | bytes accessed | tf_op | source)
XLA Modules:
  0.0 31.4 jit_solution(3025711010271779494)
XLA Ops:
  0.0 30.7 %shard_map.37 = f32[512,128]{1,0:T(8,128)S(1)} custom-call(bf16[2,64,512]{2,1,0:T(8,128)(2,1)} %bitcast.1, f32[2,512]{1,0:T(2,128)} %pivot_hbm.1, f32[512,128]{1,0:T(8,128)} %right_hbm.1), custom_call_target="tpu_custom_call" | custom-call | tf_op jit(solution)/shard_map/pallas_call | solution.py:432
  30.7 0.7 %copy.5 = f32[512,128]{1,0:T(8,128)} copy(f32[512,128]{1,0:T(8,128)S(1)} %shard_map.37) | data formatting | bytes 524288

commit v7 on v6

--- a/solution.py
+++ b/solution.py
@@ -327,7 +327,7 @@
         return remote(ref, ref, x_send.at[k, p, b], x_recv.at[k, p], {"row": diagonal_row() if b == len(bits) else flip(b)})
 
     def skips_stop(k, p):
-        return k == count - 1 and len(bits) > 1 and p >= parts // 2
+        return k == count - 1 and len(bits) > 1 and p > 0
 
     def takes(k, p, b):
         go = row >= 0
@@ -383,11 +383,17 @@
             for k in range(count):
                 step(k, p)
 
-    @pl.when(row >= count)
+    @pl.when(jnp.logical_and(row >= count, row % 2 == 0))
     def _():
         for k in range(count):
             for p in range(parts):
                 step(k, p)
+
+    @pl.when(jnp.logical_and(row >= count, row % 2 == 1))
+    def _():
+        pairs = [(k, p) for k in range(count) for p in range(parts)]
+        for k, p in sorted(pairs, key=lambda pair: (pair[1] + 2 * pair[0], -pair[0])):
+            step(k, p)
 
     out_ref[...] = work[...].T
 

time: 31.6 us -> 27.9 us (0.88)
  Pallas kernels: 30.7 us -> 26.8 us
    pallas_call x1, Pallas kernels: 30.7 us -> 26.8 us  [body(): pl.pallas_call(functools.partial(kernel, n_row, n_rhs, parts), out_shape=...]
where the time goes in v7:
time: 27.9 us; the launch traced here: 27.5 us
  Pallas kernels  26.8 us (96%)
  local copies, waits for them, and re-layouts  0.71 us (3%)
    pallas_call x1, Pallas kernels, body(): pl.pallas_call(functools.partial(kernel, n_row, n_rhs, parts), out_shape=...  26.8 us
    unnamed x1, local copies, waits for them, and re-layouts  0.71 us

profile of v7, /device:TPU:4, one launch (start us, length us, event | category | flops | bytes accessed | tf_op | source)
XLA Modules:
  0.0 27.5 jit_solution(3954062430500295602)
XLA Ops:
  0.0 26.8 %shard_map.37 = f32[512,128]{1,0:T(8,128)S(1)} custom-call(bf16[2,64,512]{2,1,0:T(8,128)(2,1)} %bitcast.1, f32[2,512]{1,0:T(2,128)} %pivot_hbm.1, f32[512,128]{1,0:T(8,128)} %right_hbm.1), custom_call_target="tpu_custom_call" | custom-call | tf_op jit(solution)/shard_map/pallas_call | solution.py:438
  26.8 0.7 %copy.5 = f32[512,128]{1,0:T(8,128)} copy(f32[512,128]{1,0:T(8,128)S(1)} %shard_map.37) | data formatting | bytes 524288

commit v8 on v7

--- a/solution.py
+++ b/solution.py
@@ -300,13 +300,15 @@
                 whole = slice(at, at + size)
                 blocks.append(diagonal(panels[row, whole, whole], row_pivots(at)))
         combine(blocks, width, lambda down, across: panels[row, down, across].astype(BF16), inverse)
+    for k in range(count):
+
+        @pl.when(row > k)
+        def _():
+            relay(k)
+
+    @pl.when(jnp.logical_and(row > 0, row < count))
+    def _():
         work[...] = product(split(work[...]), (inverse[0], inverse[1]))
-
-    for k in range(count):
-
-        @pl.when(row > k)
-        def _():
-            relay(k)
 
     for k in range(count):
 
@@ -327,7 +329,7 @@
         return remote(ref, ref, x_send.at[k, p, b], x_recv.at[k, p], {"row": diagonal_row() if b == len(bits) else flip(b)})
 
     def skips_stop(k, p):
-        return k == count - 1 and len(bits) > 1 and p > 0
+        return k == count - 1 and len(bits) > 1 and p >= parts // 4
 
     def takes(k, p, b):
         go = row >= 0
@@ -354,11 +356,16 @@
             def _():
                 send(k, p, b).start()
 
+    half = max(1, parts // 2)
+
     def step(k, p):
         at = part_rows(p)
 
         @pl.when(row == k)
         def _():
+            if k == 0 and p % half == 0:
+                group = pl.ds(p * piece, half * piece)
+                work[group, :] = product(split(work[group, :]), (inverse[0], inverse[1]))
             solved[k, 0, at, :], solved[k, 1, at, :] = split(work[at, :])
             pass_on(k, p)
 
@@ -392,7 +399,7 @@
     @pl.when(jnp.logical_and(row >= count, row % 2 == 1))
     def _():
         pairs = [(k, p) for k in range(count) for p in range(parts)]
-        for k, p in sorted(pairs, key=lambda pair: (pair[1] + 2 * pair[0], -pair[0])):
+        for k, p in sorted(pairs, key=lambda pair: (pair[1] + parts // 2 * pair[0], -pair[0])):
             step(k, p)
 
     out_ref[...] = work[...].T
@@ -428,7 +435,7 @@
     width = pivots.shape[1]
     columns = right_sides.shape[1]
     assert rows == width and n_rhs % CORES == 0
-    parts = 4 if columns % 64 == 0 else 1
+    parts = max(1, columns // 16)
     n_chip = n_rhs // CORES
     n_bits = max(1, (n_row - 1).bit_length())
     wire = BF16 if slab % 16 == 0 else F32

time: 27.9 us -> 28.7 us (1.029)
  Pallas kernels: 26.8 us -> 27.6 us
    pallas_call x1, Pallas kernels: 26.8 us -> 27.6 us  [body(): pl.pallas_call(functools.partial(kernel, n_row, n_rhs, parts), out_shape=...]
where the time goes in v8:
time: 28.7 us; the launch traced here: 28.3 us
  Pallas kernels  27.6 us (96%)
  local copies, waits for them, and re-layouts  0.71 us (2%)
    pallas_call x1, Pallas kernels, body(): pl.pallas_call(functools.partial(kernel, n_row, n_rhs, parts), out_shape=...  27.6 us
    unnamed x1, local copies, waits for them, and re-layouts  0.71 us

profile of v8, /device:TPU:4, one launch (start us, length us, event | category | flops | bytes accessed | tf_op | source)
XLA Modules:
  0.0 28.3 jit_solution(4009955999921232698)
XLA Ops:
  0.0 27.6 %shard_map.37 = f32[512,128]{1,0:T(8,128)S(1)} custom-call(bf16[2,64,512]{2,1,0:T(8,128)(2,1)} %bitcast.1, f32[2,512]{1,0:T(2,128)} %pivot_hbm.1, f32[512,128]{1,0:T(8,128)} %right_hbm.1), custom_call_target="tpu_custom_call" | custom-call | tf_op jit(solution)/shard_map/pallas_call | solution.py:445
  27.6 0.7 %copy.5 = f32[512,128]{1,0:T(8,128)} copy(f32[512,128]{1,0:T(8,128)S(1)} %shard_map.37) | data formatting | bytes 524288

commit v9 on v8

--- a/solution.py
+++ b/solution.py
@@ -435,7 +435,7 @@
     width = pivots.shape[1]
     columns = right_sides.shape[1]
     assert rows == width and n_rhs % CORES == 0
-    parts = max(1, columns // 16)
+    parts = 4 if columns % 64 == 0 else 1
     n_chip = n_rhs // CORES
     n_bits = max(1, (n_row - 1).bit_length())
     wire = BF16 if slab % 16 == 0 else F32

time: 28.7 us -> 27.9 us (0.972)
  Pallas kernels: 27.6 us -> 26.7 us
    pallas_call x1, Pallas kernels: 27.6 us -> 26.7 us  [body(): pl.pallas_call(functools.partial(kernel, n_row, n_rhs, parts), out_shape=...]
where the time goes in v9:
time: 27.9 us; the launch traced here: 27.5 us
  Pallas kernels  26.7 us (96%)
  local copies, waits for them, and re-layouts  0.71 us (3%)
    pallas_call x1, Pallas kernels, body(): pl.pallas_call(functools.partial(kernel, n_row, n_rhs, parts), out_shape=...  26.7 us
    unnamed x1, local copies, waits for them, and re-layouts  0.71 us

profile of v9, /device:TPU:4, one launch (start us, length us, event | category | flops | bytes accessed | tf_op | source)
XLA Modules:
  0.0 27.5 jit_solution(950955696322337677)
XLA Ops:
  0.0 26.7 %shard_map.37 = f32[512,128]{1,0:T(8,128)S(1)} custom-call(bf16[2,64,512]{2,1,0:T(8,128)(2,1)} %bitcast.1, f32[2,512]{1,0:T(2,128)} %pivot_hbm.1, f32[512,128]{1,0:T(8,128)} %right_hbm.1), custom_call_target="tpu_custom_call" | custom-call | tf_op jit(solution)/shard_map/pallas_call | solution.py:445
  26.8 0.7 %copy.5 = f32[512,128]{1,0:T(8,128)} copy(f32[512,128]{1,0:T(8,128)S(1)} %shard_map.37) | data formatting | bytes 524288
